TPU v7x, 256 devices: a whole 4x4x8 slice. The times are simulated.
256 devices in a mesh: vox: 32 (over z, y), col: 8 (over x, core).
Axes of the slice: x: 4, y: 4, z: 8, core: 2. Of those that a mesh axis runs over, the one named last changes fastest.
Arguments:
- start_modes: float32 [128, 131072], P('col', 'vox'), may hold values from -48 to 48
- start_dirs: float32 [128, 131072], P('col', 'vox'), may hold values from -6 to 6
- coupling: float32 [13, 131072], P(None, ('vox', 'col')), may hold values from 0.05 to 1
- relax_class: int32 [131072], P(('vox', 'col')), may hold values from 0 to 3
- relaxivity: float32 [4], replicated, may hold values from 0.5 to 4
Outputs:
- modes: float32 [128, 131072], P('col', 'vox')
- ritz: float32 [128, 128], replicated
All inputs are finite; a program needn't handle non-finite values.
Results may differ from a plain program's by a relative error of at most 0.0003.
Values sent between devices are 32-bit elements; how exact they have to be, the bound alone decides.
A program may use at most 64 MiB of HBM per device.

v0:
```python
import math
import jax
import jax.numpy as jnp
from jax import lax
from jax.sharding import PartitionSpec as P

NX = 256
NZ = 2
HALF = 13
ITERS = 2
QSTEPS = 3
offsets = [
    (a, b, c) for a in (-1, 0, 1) for b in (-1, 0, 1) for c in (-1, 0, 1) if (a, b, c) > (0, 0, 0)
]


def from_behind(block, axis, distance):
    devices = range(lax.axis_size(axis))
    route = [(i - distance, i) for i in devices if i - distance in devices]
    return lax.ppermute(block, axis, route)


def extended_2(block, sides, width):
    for axis, dim in sides:
        count = lax.axis_size(axis)
        forward = [(i, i + 1) for i in range(count - 1)]
        backward = [(target, source) for source, target in forward]
        low = lax.ppermute(
            lax.slice_in_dim(block, block.shape[dim] - width, None, axis=dim), axis, forward
        )
        high = lax.ppermute(lax.slice_in_dim(block, 0, width, axis=dim), axis, backward)
        block = jnp.concatenate([low, block, high], axis=dim)
    return block


def matmul(left, right):
    return jnp.dot(left, right, precision=lax.Precision.HIGHEST, preferred_element_type=jnp.float32)


def lower_solve(lower, rhs):
    return lax.linalg.triangular_solve(lower, rhs, left_side=True, lower=True)


def upper_solve(lower, rhs):
    return lax.linalg.triangular_solve(lower, rhs, left_side=True, lower=True, transpose_a=True)


def symmetric(matrix):
    return 0.5 * (matrix + matrix.T)


def project_pencil(gram_a, gram_b, count):
    sym_a = symmetric(gram_a)
    scales = lax.rsqrt(jnp.diagonal(gram_b) + 1e-06)
    normed_b = scales[:, None] * gram_b * scales[None, :]
    normed_a = scales[:, None] * sym_a * scales[None, :]
    lower = jnp.linalg.cholesky(normed_b)
    half_way = lower_solve(lower, normed_a)
    reduced = lower_solve(lower, half_way.T)
    shift = 2.0 * jnp.max(jnp.sum(jnp.abs(reduced), axis=1))
    iterate = jnp.eye(gram_a.shape[0], count, dtype=jnp.float32)
    for sweep_index in range(QSTEPS):
        iterate = shift * iterate - matmul(reduced, iterate)
        factor = jnp.linalg.cholesky(matmul(iterate.T, iterate))
        iterate = lower_solve(factor, iterate.T).T
    return scales[:, None] * upper_solve(lower, iterate)


def neighbour_sum(padded, coupled):
    rows_y = padded.shape[1] - 2
    rows_z = padded.shape[2] - 2
    rows_x = padded.shape[3] - 2
    total = jnp.zeros((padded.shape[0], rows_y, rows_z, rows_x), jnp.float32)
    for which, (step_y, step_z, step_x) in enumerate(offsets):
        ahead = padded[
            :,
            1 + step_y : 1 + step_y + rows_y,
            1 + step_z : 1 + step_z + rows_z,
            1 + step_x : 1 + step_x + rows_x,
        ]
        behind = padded[
            :,
            1 - step_y : 1 - step_y + rows_y,
            1 - step_z : 1 - step_z + rows_z,
            1 - step_x : 1 - step_x + rows_x,
        ]
        here = coupled[which, 1 : 1 + rows_y, 1 : 1 + rows_z, 1 : 1 + rows_x]
        back = coupled[
            which,
            1 - step_y : 1 - step_y + rows_y,
            1 - step_z : 1 - step_z + rows_z,
            1 - step_x : 1 - step_x + rows_x,
        ]
        total = total + here[None] * ahead
        total = total + back[None] * behind
    return total


def pad_plane(array):
    return jnp.pad(array, ((0, 0), (0, 0), (1, 1), (1, 1)))


def quotient(modes, images):
    total = lax.psum(matmul(modes, images.T), ("vox", "col"))
    return symmetric(total)


def on_device(start_modes, start_dirs, coupling, relax_class, relaxivity):
    local_voxels = coupling.shape[1]
    match = relax_class[:, None] == jnp.arange(relaxivity.shape[0], dtype=jnp.int32)[None, :]
    voxel_rate = jnp.sum(jnp.where(match, relaxivity[None, :], jnp.float32(0.0)), axis=1)
    damping = 1.0 / (1.0 + voxel_rate)
    own_coupling = coupling.reshape(HALF, 1, NZ, NX)
    before = from_behind(own_coupling, ("vox", "col"), 1)
    coupled = pad_plane(
        jnp.concatenate([before, own_coupling, jnp.zeros_like(own_coupling)], axis=1)
    )
    position = lax.axis_index(("vox", "col"))
    device_count = lax.axis_size(("vox", "col"))
    plane = jnp.ones((1, 1, NZ, NX), jnp.float32)
    upper_flag = (position > 0).astype(jnp.float32)
    lower_flag = (position < device_count - 1).astype(jnp.float32)
    unity = pad_plane(jnp.concatenate([upper_flag * plane, plane, lower_flag * plane], axis=1))
    degree = neighbour_sum(unity, coupled).reshape(local_voxels)
    diagonal = degree + voxel_rate

    def operate(field):
        count = field.shape[0]
        shaped = field.reshape(count, 1, NZ, NX)
        extended = extended_2(shaped, ((("vox", "col"), 1),), 1)
        padded = pad_plane(extended)
        return diagonal[None, :] * field - neighbour_sum(padded, coupled).reshape(
            count, local_voxels
        )

    modes, dirs = (
        lax.all_to_all(start_modes, "col", split_axis=1, concat_axis=0, tiled=True),
        lax.all_to_all(start_dirs, "col", split_axis=1, concat_axis=0, tiled=True),
    )
    count = modes.shape[0]
    images = operate(modes)
    dir_images = operate(dirs)
    ritz = quotient(modes, images)
    for iteration in range(ITERS):
        resid = images - matmul(ritz, modes)
        search = resid * damping[None, :]
        search_images = operate(search)
        basis = jnp.concatenate([modes, search, dirs], axis=0)
        basis_images = jnp.concatenate([images, search_images, dir_images], axis=0)
        local_a = matmul(basis, basis_images.T)
        local_b = matmul(basis, basis.T)
        gram_a, gram_b = lax.psum((local_a, local_b), ("vox", "col"))
        coeffs = project_pencil(gram_a, gram_b, count)
        modes = matmul(coeffs.T, basis)
        images = matmul(coeffs.T, basis_images)
        dirs = matmul(coeffs[count:].T, basis[count:])
        dir_images = matmul(coeffs[count:].T, basis_images[count:])
        ritz = quotient(modes, images)
    total_voxels = device_count * local_voxels
    scaled = modes * math.sqrt(total_voxels)
    modes_out = lax.all_to_all(scaled, "col", split_axis=0, concat_axis=1, tiled=True)
    return (modes_out, ritz)


def solution(mesh):
    in_specs = (P("col", "vox"), P("col", "vox"), P(None, ("vox", "col")), P(("vox", "col")), P())
    out_specs = (P("col", "vox"), P())
    return jax.shard_map(
        on_device, mesh=mesh, in_specs=in_specs, out_specs=out_specs, check_vma=False
    )
```

profile of v0, /device:TPU:1, one launch (start us, length us, event | category | flops | bytes accessed | tf_op | source)
XLA Modules:
  0.0 1733.3 jit_solution(11976527018198322847)
XLA Ops:
  7.2 1.7 copy.120
  8.8 6.6 all-to-all-start
  16.2 3.5 collective-permute-start
  22.8 1.7 copy.119
  25.2 4.1 all-to-all-start.1
  29.5 2.0 collective-permute-start.2
  31.4 3.6 collective-permute-start.1
  36.0 2.9 collective-permute-start.6
  38.9 2.6 collective-permute-start.5
  41.6 2.3 select_maximum_fusion.6
  43.9 4.5 multiply_subtract_fusion.3
  49.6 3.4 select_maximum_fusion.2
  53.1 245.1 %all-reduce.15.cloned.1.call-done = f32[128,128]{0,1:T(8,128)} async-done(((f32[128,128]{0,1:T(8,128)}), f32[128,128]{0,1:T(8,128)}) %all-reduce.15.cloned.1.call-update) | async-done | bytes 65552 | tf_op jit(solution)/shard_map/psum | solution.py:104
  301.3 2.0 collective-permute-start.4
  303.3 3.9 collective-permute-start.3
  307.2 5.4 fusion.64
  312.7 2.2 fusion.38
  314.9 2.3 select_maximum_fusion.4
  317.3 4.4 fusion.89
  322.7 2.3 fusion.14
  325.0 256.1 %all-reduce.23.cloned.1.call-done = (f32[384,384]{1,0:T(8,128)}, f32[384,384]{0,1:T(8,128)}) async-done(((f32[384,384]{1,0:T(8,128)}, f32[384,384]{0,1:T(8,128)}), (f32[384,384]{1,0:T(8,128)}, f32[384,384]{0,1:T(8,128)})) %all-reduce.23.cloned.1.call-update) | async-done | bytes 1179664 | tf_op jit(solution)/shard_map/psum | solution.py:152
  581.2 6.6 gather_fusion
  590.4 11.7 cholesky.310
  602.2 9.8 custom-call.40
  614.4 11.7 cholesky.329
  626.2 9.9 custom-call.41
  637.5 11.7 cholesky.348
  652.6 5.9 while.12
  653.2 1.3 bitcast_dynamic-update-slice_fusion.4
  658.5 29.7 %custom-call.47 = f32[3,128,128]{1,2,0:T(8,128)S(1)} custom-call(f32[3,128,128]{2,1,0:T(8,128)S(1)} %get-tuple-element.49), custom_call_target="InvertDiagBlocksLowerTriangular" | custom-call | tf_op jit(solution)/shard_map/triangular_solve/custom-call.8 | solution.py:45
  695.7 11.7 cholesky.361
  708.7 9.8 custom-call.44
  720.8 11.7 cholesky.372
  733.9 9.8 custom-call.45
  745.5 11.9 cholesky.383
  758.7 9.8 custom-call.46
  773.6 237.5 %all-reduce.17.cloned.1.call-done = f32[128,128]{1,0:T(8,128)} async-done(((f32[128,128]{1,0:T(8,128)}), f32[128,128]{1,0:T(8,128)}) %all-reduce.17.cloned.1.call-update) | async-done | bytes 65552 | tf_op jit(solution)/shard_map/psum | solution.py:104
  1013.5 1.9 collective-permute-start.8
  1015.4 3.6 collective-permute-start.7
  1019.5 2.2 fusion.36
  1022.4 2.3 select_maximum_fusion
  1024.6 4.4 fusion.39
  1029.2 2.3 fusion.12
  1031.5 259.7 %all-reduce.21.cloned.1.call-done = (f32[384,384]{1,0:T(8,128)}, f32[384,384]{0,1:T(8,128)}) async-done(((f32[384,384]{1,0:T(8,128)}, f32[384,384]{0,1:T(8,128)}), (f32[384,384]{1,0:T(8,128)}, f32[384,384]{0,1:T(8,128)})) %all-reduce.21.cloned.1.call-update) | async-done | bytes 1179664 | tf_op jit(solution)/shard_map/psum | solution.py:152
  1291.2 6.6 gather_fusion.1
  1300.6 11.7 cholesky.396
  1312.4 9.8 custom-call.48
  1324.5 11.7 cholesky.415
  1336.3 10.2 custom-call.49
  1347.8 11.7 cholesky.434
  1363.5 6.4 while.13
  1364.2 1.4 bitcast_dynamic-update-slice_fusion.5
  1366.3 1.4 bitcast_dynamic-update-slice_fusion.5
  1368.4 1.4 bitcast_dynamic-update-slice_fusion.5
  1369.9 29.7 %custom-call.55 = f32[3,128,128]{1,2,0:T(8,128)S(1)} custom-call(f32[3,128,128]{2,1,0:T(8,128)S(1)} %get-tuple-element.52), custom_call_target="InvertDiagBlocksLowerTriangular" | custom-call | tf_op jit(solution)/shard_map/triangular_solve/custom-call.8 | solution.py:45
  1407.1 11.7 cholesky.447
  1420.1 9.8 custom-call.52
  1432.0 11.7 cholesky.458
  1445.0 9.8 custom-call.53
  1456.7 11.9 cholesky.469
  1470.0 9.8 custom-call.54
  1481.7 1.4 broadcast_multiply_fusion
  1485.0 7.1 all-to-all-start.2
  1492.1 231.0 %all-reduce.19.cloned.1.call-done = f32[128,128]{1,0:T(8,128)} async-done(((f32[128,128]{1,0:T(8,128)}), f32[128,128]{1,0:T(8,128)}) %all-reduce.19.cloned.1.call-update) | async-done | bytes 65552 | tf_op jit(solution)/shard_map/psum | solution.py:104
  (313 shorter events, 78.5 us)
Async XLA Ops:
  8.8 16.4 all-to-all-start
  16.2 8.8 collective-permute-start
  25.2 10.6 all-to-all-start.1
  29.3 268.9 %all-reduce.15.cloned.1.call-start = ((), (), s32[]{:S(2)}) async-start(), calls=%async_computation.3 | async-start | bytes 131072 | tf_op jit(solution)/shard_map/psum | solution.py:104
  29.5 12.1 collective-permute-start.2
  31.4 10.1 collective-permute-start.1
  35.1 13.3 copy-start.21
  35.1 13.3 copy-start.23
  35.1 13.3 copy-start.25
  35.1 13.3 copy-start.27
  35.2 13.3 copy-start.29
  35.2 13.3 copy-start.31
  35.2 13.3 copy-start.33
  35.8 17.2 copy-start.35
  36.0 12.5 copy-start.15
  36.0 13.6 collective-permute-start.6
  38.9 10.7 collective-permute-start.5
  49.6 531.6 %all-reduce.23.cloned.1.call-start = ((), (), s32[]{:S(2)}) async-start(), calls=%async_computation.7 | async-start | bytes 2359296 | tf_op jit(solution)/shard_map/psum | solution.py:152
  49.6 3.4 copy-start.14
  301.3 13.6 copy-start.16
  301.3 13.6 collective-permute-start.4
  303.3 11.6 collective-permute-start.3
  312.6 4.6 copy-start.22
  312.6 4.6 copy-start.24
  312.6 4.6 copy-start.26
  312.6 4.6 copy-start.28
  312.6 4.6 copy-start.30
  312.6 4.6 copy-start.32
  312.7 4.6 copy-start.34
  317.3 4.5 copy-start.36
  321.9 0.7 copy-start.6
  321.9 0.8 copy-start.8
  325.0 686.1 %all-reduce.17.cloned.1.call-start = ((), (), s32[]{:S(2)}) async-start(), calls=%async_computation.4 | async-start | bytes 131072 | tf_op jit(solution)/shard_map/psum | solution.py:104
  581.2 6.6 copy-start.2
  581.2 7.7 copy-start
  590.4 11.7 copy-start.12
  744.1 26.5 %copy-start.7 = (f32[128,512]{1,0:T(8,128)S(1)}, f32[128,512]{1,0:T(8,128)}, u32[]{:S(2)}) copy-start(f32[128,512]{1,0:T(8,128)} %copy-done.6) | copy-start | bytes 786436
  744.1 26.5 %copy-start.9 = (f32[128,512]{1,0:T(8,128)S(1)}, f32[128,512]{1,0:T(8,128)}, u32[]{:S(2)}) copy-start(f32[128,512]{1,0:T(8,128)} %copy-done.8) | copy-start | bytes 786436
  770.2 241.8 %copy-start.37 = (f32[512]{0:T(512)S(1)}, f32[512]{0:T(512)}, u32[]{:S(2)}) copy-start(f32[512]{0:T(512)} %get-tuple-element.163) | copy-start | bytes 6148
  771.3 257.8 %copy-start.4 = (f32[128,512]{1,0:T(8,128)}, f32[128,512]{1,0:T(8,128)S(1)}, u32[]{:S(2)}) copy-start(f32[128,512]{1,0:T(8,128)S(1)} %fusion.13) | copy-start | bytes 786436
  773.1 518.2 %all-reduce.21.cloned.1.call-start = ((), (), s32[]{:S(2)}) async-start(), calls=%async_computation.6 | async-start | bytes 2359296 | tf_op jit(solution)/shard_map/psum | solution.py:152
  773.6 255.6 %copy-start.10 = (f32[128,512]{1,0:T(8,128)}, f32[128,512]{1,0:T(8,128)S(1)}, u32[]{:S(2)}) copy-start(f32[128,512]{1,0:T(8,128)S(1)} %fusion.15) | copy-start | bytes 786436
  1013.5 8.3 collective-permute-start.8
  1015.4 6.9 collective-permute-start.7
  1019.5 9.7 copy-start.17
  1029.2 268.7 %copy-start.19 = (f32[128,512]{1,0:T(8,128)}, f32[128,512]{1,0:T(8,128)S(1)}, u32[]{:S(2)}) copy-start(f32[128,512]{1,0:T(8,128)S(1)} %multiply_subtract_fusion) | copy-start | bytes 786436
  1031.5 691.6 %all-reduce.19.cloned.1.call-start = ((), (), s32[]{:S(2)}) async-start(), calls=%async_computation.5 | async-start | bytes 131072 | tf_op jit(solution)/shard_map/psum | solution.py:104
  1291.2 6.7 copy-start.3
  1291.2 7.7 copy-start.1
  1300.5 11.7 copy-start.13
  1454.8 26.9 %copy-start.11 = (f32[128,512]{1,0:T(8,128)S(1)}, f32[128,512]{1,0:T(8,128)}, u32[]{:S(2)}) copy-start(f32[128,512]{1,0:T(8,128)} %copy-done.10) | copy-start | bytes 786436
  1455.9 27.2 %copy-start.5 = (f32[128,512]{1,0:T(8,128)S(1)}, f32[128,512]{1,0:T(8,128)}, u32[]{:S(2)}) copy-start(f32[128,512]{1,0:T(8,128)} %copy-done.4) | copy-start | bytes 786436
  1455.9 27.2 %copy-start.18 = (f32[128,512]{1,0:T(8,128)S(1)}, f32[128,512]{1,0:T(8,128)}, u32[]{:S(2)}) copy-start(f32[128,512]{1,0:T(8,128)} %copy-done.17) | copy-start | bytes 786436
  1455.9 27.2 %copy-start.20 = (f32[128,512]{1,0:T(8,128)S(1)}, f32[128,512]{1,0:T(8,128)}, u32[]{:S(2)}) copy-start(f32[128,512]{1,0:T(8,128)} %copy-done.19) | copy-start | bytes 786436
  1485.0 240.7 %all-to-all-start.2 = ((f32[8,16,512]{2,1,0:T(8,128)}), f32[8,16,512]{2,1,0:T(8,128)S(1)}, u32[]{:S(2)}, u32[]{:S(2)}) async-start(f32[8,16,512]{2,1,0:T(8,128)} %bitcast.87), calls=%async_computation.2 | async-start | bytes 524288 | tf_op jit(solution)/shard_map/all_to_all | solution.py:161
Sparse Core Ops, SparseCore 0:
  49.7 248.4 all-reduce.14
  325.1 256.0 all-reduce.22
  773.2 237.8 all-reduce.16
  1031.6 259.5 all-reduce.20
  1485.1 237.9 all-reduce.18
where the time goes:
time: 1740 us; the launch traced here: 1730 us
  waiting for transfers between devices  1230 us (71%)
  other arithmetic  348 us (20%)
  matrix products  48.7 us (3%)
  starting transfers between devices  44.1 us (3%)
  local copies, waits for them, and re-layouts  41.4 us (2%)
  between operations  21 us (1%)
    psum x3, waiting for transfers between devices, quotient(): total = lax.psum(matmul(modes, images.T), ('vox', 'col'))  714 us
    psum x2, waiting for transfers between devices, on_device(): gram_a, gram_b = lax.psum((local_a, local_b), ('vox', 'col'))  516 us
    another operation x21, other arithmetic, project_pencil(): lower = jnp.linalg.cholesky(normed_b)  114 us
    another operation x18, other arithmetic, project_pencil(): factor = jnp.linalg.cholesky(matmul(iterate.T, iterate))  74.7 us
    another operation x12, other arithmetic, lower_solve(): return lax.linalg.triangular_solve(lower, rhs, left_side=True, lower=True)  62.8 us
    another operation x5, other arithmetic, upper_solve(): lax.linalg.triangular_solve(lower, rhs, left_side=True, lower=True, trans...  59.5 us
  transfers between devices with their start and end apart: 17, of which 6 were waited for; matrix products, arithmetic and copies ran while one was open for 2% of the time, Pallas kernels for 0%

commit v1 on v0

--- a/solution.py
+++ b/solution.py
@@ -101,7 +101,7 @@
 
 
 def quotient(modes, images):
-    total = lax.psum(matmul(modes, images.T), ("vox", "col"))
+    total = jnp.sum(lax.all_gather(matmul(modes, images.T), ("vox", "col")), axis=0)
     return symmetric(total)
 
 

time: 1740 us -> 1430 us (0.82)
  waiting for transfers between devices: 1230 us -> 890 us
  other arithmetic: 348 us -> 369 us
    psum x3 -> x0, waiting for transfers between devices: 714 us -> none  [quotient(): total = lax.psum(matmul(modes, images.T), ('vox', 'col'))]
    all_gather x0 -> x3, waiting for transfers between devices: none -> 352 us  [quotient(): lax.all_gather(matmul(modes, images.T), ('vox', 'col'))]
    reduce_sum x0 -> x3, other arithmetic: none -> 21.2 us  [quotient(): jnp.sum(lax.all_gather(matmul(modes, images.T), ('vox', 'col')), axis=0)]
  transfers between devices with their start and end apart: 17 -> 16, of which waited for: 6 -> 12; matrix products, arithmetic and copies ran while one was open for 2% -> 2% of each run, Pallas kernels for 0% -> 0%
where the time goes in v1:
time: 1430 us; the launch traced here: 1420 us
  waiting for transfers between devices  890 us (62%)
  other arithmetic  369 us (26%)
  local copies, waits for them, and re-layouts  49.2 us (3%)
  matrix products  42.5 us (3%)
  starting transfers between devices  36.1 us (3%)
  between operations  21.4 us (1%)
    psum x2, waiting for transfers between devices, on_device(): gram_a, gram_b = lax.psum((local_a, local_b), ('vox', 'col'))  515 us
    all_gather x3, waiting for transfers between devices, quotient(): lax.all_gather(matmul(modes, images.T), ('vox', 'col'))  352 us
    another operation x21, other arithmetic, project_pencil(): lower = jnp.linalg.cholesky(normed_b)  114 us
    another operation x18, other arithmetic, project_pencil(): factor = jnp.linalg.cholesky(matmul(iterate.T, iterate))  74.7 us
    another operation x12, other arithmetic, lower_solve(): return lax.linalg.triangular_solve(lower, rhs, left_side=True, lower=True)  62.8 us
    another operation x5, other arithmetic, upper_solve(): lax.linalg.triangular_solve(lower, rhs, left_side=True, lower=True, trans...  59.5 us
  transfers between devices with their start and end apart: 16, of which 12 were waited for; matrix products, arithmetic and copies ran while one was open for 2% of the time, Pallas kernels for 0%

profile of v1, /device:TPU:1, one launch (start us, length us, event | category | flops | bytes accessed | tf_op | source)
XLA Modules:
  0.0 1421.7 jit_solution(4915920932251080061)
XLA Ops:
  7.9 4.5 collective-permute-start
  14.1 4.1 all-to-all-start
  22.0 2.8 all-to-all-done
  25.0 3.1 collective-permute-start.1
  31.4 4.4 collective-permute-done.2
  35.8 2.3 select_maximum_fusion.6
  38.1 4.5 multiply_subtract_fusion.3
  44.6 7.2 all-to-all-start.1
  51.8 6.5 all-to-all-done.1
  58.5 3.1 collective-permute-start.5
  64.9 4.7 collective-permute-done.6
  70.3 3.2 select_maximum_fusion.2
  73.5 116.6 %all-gather.7.cloned.1.call-done = f32[32768,128]{0,1:T(8,128)} async-done(((f32[128,128]{0,1:T(8,128)}), f32[32768,128]{0,1:T(8,128)}) %all-gather.7.cloned.1.call-update) | async-done | bytes 16777232 | tf_op jit(solution)/shard_map/all_gather | solution.py:104
  190.1 14.1 copy.147
  204.2 8.0 bitcast_reduce_fusion
  216.3 2.7 collective-permute-start.4
  219.0 5.5 fusion.64
  224.8 2.2 fusion.38
  227.0 2.3 select_maximum_fusion.4
  229.6 4.4 fusion.89
  234.9 2.3 fusion.14
  237.3 255.8 %all-reduce.14.cloned.1.call-done = (f32[384,384]{1,0:T(8,128)}, f32[384,384]{0,1:T(8,128)}) async-done(((f32[384,384]{1,0:T(8,128)}, f32[384,384]{0,1:T(8,128)}), (f32[384,384]{1,0:T(8,128)}, f32[384,384]{0,1:T(8,128)})) %all-reduce.14.cloned.1.call-update) | async-done | bytes 1179664 | tf_op jit(solution)/shard_map/psum | solution.py:152
  493.1 2.2 copy.98
  495.3 3.9 gather_fusion
  500.8 11.7 cholesky.310
  512.6 9.8 custom-call.40
  523.0 11.7 cholesky.329
  534.8 10.0 custom-call.41
  545.2 11.7 cholesky.348
  560.3 6.2 while.12
  566.5 29.7 %custom-call.47 = f32[3,128,128]{1,2,0:T(8,128)S(1)} custom-call(f32[3,128,128]{2,1,0:T(8,128)S(1)} %get-tuple-element.49), custom_call_target="InvertDiagBlocksLowerTriangular" | custom-call | tf_op jit(solution)/shard_map/triangular_solve/custom-call.8 | solution.py:45
  603.7 11.7 cholesky.361
  616.8 9.8 custom-call.44
  628.9 11.7 cholesky.372
  641.9 9.8 custom-call.45
  653.6 11.9 cholesky.383
  666.8 9.8 custom-call.46
  681.6 124.7 %all-gather.9.cloned.1.call-done = f32[32768,128]{1,0:T(8,128)} async-done(((f32[128,128]{1,0:T(8,128)}), f32[32768,128]{1,0:T(8,128)}) %all-gather.9.cloned.1.call-update) | async-done | bytes 16777232 | tf_op jit(solution)/shard_map/all_gather | solution.py:104
  806.4 6.6 reduce_sum.60
  813.6 3.2 collective-permute-start.7
  819.2 2.3 fusion.36
  821.5 3.0 collective-permute-done.8
  824.5 2.3 select_maximum_fusion
  826.8 4.4 fusion.39
  831.3 2.3 fusion.12
  833.7 259.0 %all-reduce.12.cloned.1.call-done = (f32[384,384]{1,0:T(8,128)}, f32[384,384]{0,1:T(8,128)}) async-done(((f32[384,384]{1,0:T(8,128)}, f32[384,384]{0,1:T(8,128)}), (f32[384,384]{1,0:T(8,128)}, f32[384,384]{0,1:T(8,128)})) %all-reduce.12.cloned.1.call-update) | async-done | bytes 1179664 | tf_op jit(solution)/shard_map/psum | solution.py:152
  1092.7 2.2 copy.113
  1095.0 3.7 gather_fusion.1
  1100.2 11.7 cholesky.396
  1112.0 9.8 custom-call.48
  1122.4 11.7 cholesky.415
  1135.5 10.2 custom-call.49
  1146.2 11.7 cholesky.434
  1160.6 6.4 while.13
  1166.9 29.7 %custom-call.55 = f32[3,128,128]{1,2,0:T(8,128)S(1)} custom-call(f32[3,128,128]{2,1,0:T(8,128)S(1)} %get-tuple-element.52), custom_call_target="InvertDiagBlocksLowerTriangular" | custom-call | tf_op jit(solution)/shard_map/triangular_solve/custom-call.8 | solution.py:45
  1204.1 11.7 cholesky.447
  1217.1 9.8 custom-call.52
  1229.0 11.7 cholesky.458
  1242.0 9.8 custom-call.53
  1253.7 11.9 cholesky.469
  1267.0 9.8 custom-call.54
  1282.2 13.4 all_to_all.57
  1296.3 111.2 %all-gather.11.cloned.1.call-done = f32[32768,128]{1,0:T(8,128)} async-done(((f32[128,128]{1,0:T(8,128)}), f32[32768,128]{1,0:T(8,128)}) %all-gather.11.cloned.1.call-update) | async-done | bytes 16777232 | tf_op jit(solution)/shard_map/all_gather | solution.py:104
  1407.4 6.6 reduce_sum.62
  (373 shorter events, 86.1 us)
Async XLA Ops:
  7.9 14.0 collective-permute-start
  14.1 10.6 all-to-all-start
  18.3 171.8 %all-gather.7.cloned.1.call-start = ((), (), s32[]{:S(2)}) async-start(), calls=%async_computation.3 | async-start | bytes 16842752 | tf_op jit(solution)/shard_map/all_gather | solution.py:104
  21.7 20.9 %copy-start.18 = (f32[2,256]{1,0:T(2,128)}, f32[2,256]{1,0:T(2,128)S(1)}, u32[]{:S(2)}) copy-start(f32[2,256]{1,0:T(2,128)S(1)} %mul.1121) | copy-start | bytes 6148
  21.7 20.9 %copy-start.20 = (f32[2,256]{1,0:T(2,128)}, f32[2,256]{1,0:T(2,128)S(1)}, u32[]{:S(2)}) copy-start(f32[2,256]{1,0:T(2,128)S(1)} %mul.1127) | copy-start | bytes 6148
  21.7 20.9 %copy-start.22 = (f32[2,256]{1,0:T(2,128)}, f32[2,256]{1,0:T(2,128)S(1)}, u32[]{:S(2)}) copy-start(f32[2,256]{1,0:T(2,128)S(1)} %mul.1073) | copy-start | bytes 6148
  21.7 20.9 %copy-start.24 = (f32[2,256]{1,0:T(2,128)}, f32[2,256]{1,0:T(2,128)S(1)}, u32[]{:S(2)}) copy-start(f32[2,256]{1,0:T(2,128)S(1)} %mul.1079) | copy-start | bytes 6148
  21.8 20.8 %copy-start.26 = (f32[2,256]{1,0:T(2,128)}, f32[2,256]{1,0:T(2,128)S(1)}, u32[]{:S(2)}) copy-start(f32[2,256]{1,0:T(2,128)S(1)} %mul.1085) | copy-start | bytes 6148
  21.8 20.8 %copy-start.28 = (f32[2,256]{1,0:T(2,128)}, f32[2,256]{1,0:T(2,128)S(1)}, u32[]{:S(2)}) copy-start(f32[2,256]{1,0:T(2,128)S(1)} %mul.1091) | copy-start | bytes 6148
  21.8 20.8 %copy-start.30 = (f32[2,256]{1,0:T(2,128)}, f32[2,256]{1,0:T(2,128)S(1)}, u32[]{:S(2)}) copy-start(f32[2,256]{1,0:T(2,128)S(1)} %mul.1097) | copy-start | bytes 6148
  21.8 20.8 %copy-start.32 = (f32[2,256]{1,0:T(2,128)}, f32[2,256]{1,0:T(2,128)S(1)}, u32[]{:S(2)}) copy-start(f32[2,256]{1,0:T(2,128)S(1)} %mul.1103) | copy-start | bytes 6148
  21.9 20.8 %copy-start.34 = (f32[2,256]{1,0:T(2,128)}, f32[2,256]{1,0:T(2,128)S(1)}, u32[]{:S(2)}) copy-start(f32[2,256]{1,0:T(2,128)S(1)} %mul.1133) | copy-start | bytes 6148
  21.9 20.8 %copy-start.36 = (f32[2,256]{1,0:T(2,128)}, f32[2,256]{1,0:T(2,128)S(1)}, u32[]{:S(2)}) copy-start(f32[2,256]{1,0:T(2,128)S(1)} %mul.1139) | copy-start | bytes 6148
  21.9 20.8 %copy-start.38 = (f32[2,256]{1,0:T(2,128)}, f32[2,256]{1,0:T(2,128)S(1)}, u32[]{:S(2)}) copy-start(f32[2,256]{1,0:T(2,128)S(1)} %slice_bitcast_fusion.24) | copy-start | bytes 6148
  25.0 6.4 collective-permute-start.1
  28.1 7.7 collective-permute-start.2
  30.1 12.6 copy-start.40
  30.1 12.6 copy-start.42
  30.1 12.6 copy-start.44
  30.1 12.6 copy-start.46
  30.1 12.6 copy-start.48
  30.1 12.6 copy-start.50
  30.2 12.6 copy-start.52
  30.2 12.6 copy-start.54
  30.2 12.6 copy-start.56
  30.2 12.6 copy-start.58
  30.2 12.6 copy-start.60
  30.2 12.6 copy-start.62
  38.1 5.8 copy-start.17
  44.6 13.7 all-to-all-start.1
  51.8 441.3 %all-reduce.14.cloned.1.call-start = ((), (), s32[]{:S(2)}) async-start(), calls=%async_computation.7 | async-start | bytes 2359296 | tf_op jit(solution)/shard_map/psum | solution.py:152
  58.5 6.4 copy-start.12
  58.5 6.4 collective-permute-start.5
  61.6 8.0 collective-permute-start.6
  64.9 139.3 %copy-start.10 = (f32[128,1,2,256]{3,2,0,1:T(2,128)}, f32[128,1,2,256]{3,2,0,1:T(2,128)S(1)}, u32[]{:S(2)}) copy-start(f32[128,1,2,256]{3,2,0,1:T(2,128)S(1)} %collective-permute-done.5) | copy-start | bytes 786436
  214.3 12.7 copy-start.13
  214.3 12.7 collective-permute-start.3
  216.3 10.7 collective-permute-start.4
  224.5 4.8 copy-start.19
  224.6 4.8 copy-start.21
  224.6 4.8 copy-start.23
  224.6 4.8 copy-start.25
  224.6 4.8 copy-start.27
  224.6 4.8 copy-start.29
  224.6 4.8 copy-start.31
  224.6 4.8 copy-start.33
  224.6 4.8 copy-start.35
  224.6 4.8 copy-start.37
  224.6 4.8 copy-start.39
  237.2 569.2 %all-gather.9.cloned.1.call-start = ((), (), s32[]{:S(2)}) async-start(), calls=%async_computation.4 | async-start | bytes 16842752 | tf_op jit(solution)/shard_map/all_gather | solution.py:104
  493.1 6.2 copy-start.2
  653.0 26.4 %copy-start.5 = (f32[128,512]{1,0:T(8,128)S(1)}, f32[128,512]{1,0:T(8,128)}, u32[]{:S(2)}) copy-start(f32[128,512]{1,0:T(8,128)} %copy-done.4) | copy-start | bytes 786436
  653.0 26.4 %copy-start.7 = (f32[128,512]{1,0:T(8,128)S(1)}, f32[128,512]{1,0:T(8,128)}, u32[]{:S(2)}) copy-start(f32[128,512]{1,0:T(8,128)} %copy-done.6) | copy-start | bytes 786436
  681.1 411.6 %all-reduce.12.cloned.1.call-start = ((), (), s32[]{:S(2)}) async-start(), calls=%async_computation.6 | async-start | bytes 2359296 | tf_op jit(solution)/shard_map/psum | solution.py:152
  681.6 149.7 %copy-start.8 = (f32[128,512]{1,0:T(8,128)}, f32[128,512]{1,0:T(8,128)S(1)}, u32[]{:S(2)}) copy-start(f32[128,512]{1,0:T(8,128)S(1)} %fusion.15) | copy-start | bytes 786436
  806.4 6.7 copy-start.66
  813.6 7.9 collective-permute-start.7
  816.8 7.7 collective-permute-start.8
  819.2 12.1 copy-start.14
  831.3 267.3 %copy-start.16 = (f32[128,512]{1,0:T(8,128)}, f32[128,512]{1,0:T(8,128)S(1)}, u32[]{:S(2)}) copy-start(f32[128,512]{1,0:T(8,128)S(1)} %multiply_subtract_fusion) | copy-start | bytes 786436
  833.6 573.8 %all-gather.11.cloned.1.call-start = ((), (), s32[]{:S(2)}) async-start(), calls=%async_computation.5 | async-start | bytes 16842752 | tf_op jit(solution)/shard_map/all_gather | solution.py:104
  1092.7 6.0 copy-start.3
  1251.9 26.8 %copy-start.15 = (f32[128,512]{1,0:T(8,128)S(1)}, f32[128,512]{1,0:T(8,128)}, u32[]{:S(2)}) copy-start(f32[128,512]{1,0:T(8,128)} %copy-done.14) | copy-start | bytes 786436
  1253.1 27.3 %copy-start.9 = (f32[128,512]{1,0:T(8,128)S(1)}, f32[128,512]{1,0:T(8,128)}, u32[]{:S(2)}) copy-start(f32[128,512]{1,0:T(8,128)} %copy-done.8) | copy-start | bytes 786436
  (19 other events, 69.0 us)
Sparse Core Ops, SparseCore 0:
  44.0 146.0 all-gather.6
  237.3 255.7 all-reduce.13
  681.2 125.1 all-gather.8
  833.7 258.9 all-reduce.11
  1282.3 125.0 all-gather.10
